TPU v7x, 32 devices: a whole 2x2x4 slice. The times are simulated.
32 devices in a mesh: groups: 2 (over x), expert: 16 (over z, y, core).
Axes of the slice: x: 2, y: 2, z: 4, core: 2. Of those that a mesh axis runs over, the one named last changes fastest.
Arguments:
- hidden: bfloat16 [8192, 6, 1536], P(('groups', 'expert')), parts along dimension 0, may hold values from -6 to 6
- out_grad: bfloat16 [8192, 5120], P(('groups', 'expert')), parts along dimension 0, may hold values from -6 to 6
- gate_weights: float32 [8192, 6], P(('groups', 'expert')), parts along dimension 0, may hold values from 0.02 to 0.5
- expert_ids: int32 [8192, 6], P(('groups', 'expert')), parts along dimension 0, may hold values from 0 to 31, all different within a row; in each aligned block of 256 rows (0 to 255, 256 to 511, ...) at most 64 rows name the same one
- example_ids: int32 [8192], P(('groups', 'expert')), parts along dimension 0, may hold values from 0 to 31, as said below
- query_ids: int32 [64], P('groups'), parts along dimension 0, may hold values from 0 to 31
- in_factor: bfloat16 [32, 1536, 64], P('expert'), may hold values from -0.15625 to 0.15625
- out_factor: bfloat16 [5120, 64], replicated, may hold values from -0.078125 to 0.078125
Outputs:
- sketch: float32 [64, 4096], P(('groups', 'expert')), parts along dimension 0
- scores: float32 [64, 32], P(('groups', 'expert')), parts along dimension 0
There are 2 independent parts, one for each index of `groups`. A program takes and returns all parts, laid end to end along the dimension named above; an argument that names none is the same for every part. Nothing has to cross between parts.
Inputs may be any that keep to these rules, and one draw needn't show every extreme that they name: `expert_ids`: each row names 6 different experts; in each aligned block of 256 rows no expert is named by more than 64 rows, a bound that some block reaches. `example_ids`: in aligned block b of 256 tokens the ids never fall and take every value from b * 2 to b * 2 + 1.
All inputs are finite; a program needn't handle non-finite values.
Results may differ from a plain program's by a relative error of at most 0.0003.
Values may be sent and summed in bfloat16 or wider, within the bound.
A program may use at most 128 MiB of HBM per device.

v0:
```python
import jax
import jax.numpy as jnp
from jax import lax
from jax.sharding import PartitionSpec as P

EX_DEV = 2


sketch_scale = 0.125
score_scale = 1.0 / 512.0
epsilon = 1e-06


def on_device(
    hidden, out_grad, gate_weights, expert_ids, example_ids, query_ids, in_factor, out_factor
):
    devices = lax.axis_size("expert")
    tok_rows, top_count, feat_width = hidden.shape
    exp_local = in_factor.shape[0]
    rank_width = out_factor.shape[1]
    experts_all = exp_local * devices
    capacity = 4 * tok_rows * top_count // (3 * experts_all)
    slot_count = tok_rows * top_count
    slot_expert = expert_ids.reshape(slot_count)
    onehot = (slot_expert[:, None] == jnp.arange(experts_all, dtype=jnp.int32)[None, :]).astype(
        jnp.bfloat16
    )
    row_index = lax.broadcasted_iota(jnp.int32, (slot_count, slot_count), 0)
    col_index = lax.broadcasted_iota(jnp.int32, (slot_count, slot_count), 1)
    below_mask = (row_index > col_index).astype(jnp.bfloat16)
    before = jnp.dot(below_mask, onehot, preferred_element_type=jnp.float32)
    slot_rank = jnp.sum(before * onehot.astype(jnp.float32), axis=1).astype(jnp.int32)
    slot_place = slot_expert * capacity + slot_rank
    grad_proj = jnp.dot(out_grad, out_factor, preferred_element_type=jnp.float32)
    grad_slot = jnp.repeat(grad_proj, top_count, axis=0)
    example_local = jnp.repeat(example_ids % EX_DEV, top_count)
    weight_slot = (example_local[:, None] == jnp.arange(EX_DEV, dtype=jnp.int32)[None, :]).astype(
        jnp.float32
    )
    weight_slot = weight_slot * gate_weights.reshape(slot_count, 1)
    hidden_buffer = jnp.zeros((experts_all * capacity, feat_width), jnp.bfloat16)
    hidden_buffer = hidden_buffer.at[slot_place].set(hidden.reshape(slot_count, feat_width))
    hidden_buffer = hidden_buffer.reshape(experts_all, capacity, feat_width)
    in_proj = jnp.einsum(
        "ecf,efk->eck",
        hidden_buffer,
        lax.all_gather(in_factor, "expert", axis=0, tiled=True),
        preferred_element_type=jnp.float32,
    )
    slot_proj = in_proj.reshape(experts_all * capacity, rank_width)[slot_place]
    sketch = jnp.einsum(
        "rx,ri,rj->xij", weight_slot, slot_proj, grad_slot, precision=lax.Precision.HIGHEST
    )
    sketch = sketch.reshape(EX_DEV, rank_width * rank_width) * sketch_scale
    pieces = lax.all_gather(sketch, "expert", axis=0, tiled=True)
    chooser = (query_ids[:, None] == jnp.arange(pieces.shape[0], dtype=jnp.int32)[None, :]).astype(
        jnp.float32
    )
    queries = jnp.dot(chooser, pieces, precision=lax.Precision.HIGHEST)
    row_scale = lax.rsqrt(jnp.mean(sketch * sketch, axis=1) + epsilon)
    query_scale = lax.rsqrt(jnp.mean(queries * queries, axis=1) + epsilon)
    scores = jnp.dot(sketch, queries.T, precision=lax.Precision.HIGHEST)
    scores = scores * row_scale[:, None] * query_scale[None, :] * score_scale
    return (sketch, scores)


def solution(mesh):
    in_specs = (
        P(("groups", "expert"), None, None),
        P(("groups", "expert"), None),
        P(("groups", "expert"), None),
        P(("groups", "expert"), None),
        P(("groups", "expert")),
        P("groups"),
        P("expert", None, None),
        P(),
    )
    out_specs = (P(("groups", "expert"), None), P(("groups", "expert"), None))
    return jax.shard_map(
        on_device, mesh=mesh, in_specs=in_specs, out_specs=out_specs, check_vma=False
    )
```

profile of v0, /device:TPU:0, one launch (start us, length us, event | category | flops | bytes accessed | tf_op | source)
XLA Modules:
  0.0 123.4 jit_solution(11349060898565888185)
XLA Ops:
  7.2 0.0 copy-start
  7.2 0.0 all-gather.3.cloned.1.call-start
  7.2 0.7 all-gather.3.cloned.1.call-update
  7.9 0.9 copy.19
  8.8 0.1 eq.45
  8.9 0.9 fusion.4
  9.9 0.6 convert_element_type.24
  10.5 0.7 broadcast_multiply_fusion
  11.2 0.1 copy.18
  11.3 0.7 mul.75
  12.1 7.7 %copy.20 = bf16[256,6,1536]{2,1,0:T(8,128)(2,1)} copy(bf16[256,6,1536]{2,0,1:T(8,128)(2,1)} %param.8) | data formatting | bytes 9437184 | tf_op args[0]
  19.8 8.5 %reshape.83 = bf16[1536,1536]{1,0:T(8,128)(2,1)} reshape(bf16[256,6,1536]{2,1,0:T(8,128)(2,1)} %copy.20) | data formatting | bytes 9437184 | tf_op jit(solution)/shard_map/reshape | solution.py:42
  28.3 0.8 fusion.18
  29.1 1.1 broadcast_in_dim.8
  30.2 1.3 %reshape.70 = f32[1536,64]{1,0:T(8,128)S(1)} reshape(f32[256,6,64]{2,1,0:T(8,128)} %broadcast_in_dim.8) | data formatting | bytes 786432 | tf_op jit(solution)/shard_map/reshape | solution.py:35
  31.5 0.1 broadcast_in_dim.7
  31.6 0.1 eq.49
  31.8 0.1 copy.22
  31.9 0.1 mul.77
  32.1 0.7 fusion.15
  32.8 12.4 %scatter_custom_fusion = bf16[2048,1536]{1,0:T(8,128)(2,1)} fusion(s32[1536]{0:T(1024)S(1)} %fusion.15, bf16[1536,1536]{1,0:T(8,128)(2,1)} %reshape.83, bf16[]{:T(256)} %constant.11.clone.1), kind=kCustom, calls=%fused_computation.4 | custom fusion | bytes 6291968 | tf_op jit(solution)/shard_map/scatter | solution.py:42
  45.2 29.6 %all-gather.3.cloned.1.call-done = bf16[32,1536,64]{1,2,0:T(8,128)(2,1)} async-done(((bf16[2,1536,64]{1,2,0:T(8,128)(2,1)}), bf16[32,1536,64]{1,2,0:T(8,128)(2,1)}) %all-gather.3.cloned.1.call-update) | async-done | bytes 6291472 | tf_op jit(solution)/shard_map/all_gather | solution.py:47
  74.9 7.4 %fusion.17 = f32[32,64,64]{2,1,0:T(8,128)} fusion(bf16[32,64,1536]{2,1,0:T(8,128)(2,1)} %bitcast.16, bf16[32,1536,64]{1,2,0:T(8,128)(2,1)} %all-gather.3.cloned.1.call-done), kind=kOutput, calls=%fused_computation.35 | convolution fusion | flops 402653184 | bytes 13107200 | tf_op jit(solution)/shard_map/ecf,efk->eck/dot_general | solution.py:44
  82.3 4.9 %gather_fusion = f32[1536,64]{1,0:T(8,128)} fusion(f32[2048,64]{1,0:T(8,128)} %bitcast.15, s32[2048]{0:T(1024)S(1)} %pad_clamp_fusion), kind=kCustom, calls=%fused_computation | custom fusion | bytes 792576 | tf_op jit(solution)/shard_map/gather | solution.py:50
  87.2 2.1 %copy.21 = f32[1536,64]{0,1:T(8,128)} copy(f32[1536,64]{1,0:T(8,128)} %gather_fusion) | data formatting | bytes 786432 | tf_op jit(solution)/shard_map/gather | solution.py:50
  89.3 2.0 %multiply_reduce_fusion.1 = (f32[2]{0:T(128)S(1)}, f32[64,2,64]{2,0,1:T(8,128)S(1)}) fusion(f32[1536,64]{1,0:T(8,128)S(1)} %reshape.70, f32[1536,2]{0,1:T(2,128)S(1)} %compare_select_fusion.1, f32[1536,64]{0,1:T(8,128)} %copy.21), kind=kOutput, calls=%fused_computation.20 | convolution fusion | flops 151216128 | bytes 831496 | tf_op jit(solution)/shard_map/rx,ri,rj->xij/dot_general | solution.py:51
  91.3 0.1 reshape.87
  91.4 0.1 mul.83
  91.5 22.0 %all-gather = f32[16,2,4096]{2,1,0:T(2,128)} all-gather(f32[1,2,4096]{2,1,0:T(2,128)S(1)} %reshape.87), channel_id=1, replica_groups=mesh['groups'=2,'expert'=16] {'expert'}, dimensions={0}, use_global_device_ids=true | all-gather | bytes 557056 | tf_op jit(solution)/shard_map/all_gather | solution.py:55
  113.5 1.4 %reshape.88 = f32[32,4096]{1,0:T(8,128)S(1)} reshape(f32[16,2,4096]{2,1,0:T(2,128)} %all-gather) | data formatting | bytes 1048576
  114.9 0.5 multiply_reduce_fusion
  115.5 1.1 fusion.6
  (16 shorter events, 0.1 us)
Async XLA Ops:
  7.2 21.1 %copy-start = (bf16[256,5120]{1,0:T(8,128)(2,1)S(1)}, bf16[256,5120]{1,0:T(8,128)(2,1)}, u32[]{:S(2)}) copy-start(bf16[256,5120]{1,0:T(8,128)(2,1)} %param.9) | copy-start | bytes 7864324
  7.2 67.7 %all-gather.3.cloned.1.call-start = ((), (), s32[]{:S(2)}) async-start(), calls=%async_computation | async-start | bytes 6684672 | tf_op jit(solution)/shard_map/all_gather | solution.py:47
  19.7 8.5 %copy-start.1 = (bf16[5120,64]{0,1:T(8,128)(2,1)S(1)}, bf16[5120,64]{0,1:T(8,128)(2,1)}, u32[]{:S(2)}) copy-start(bf16[5120,64]{0,1:T(8,128)(2,1)} %param.15) | copy-start | bytes 1966084
  19.8 11.8 %copy-start.4 = (s32[256]{0:T(256)S(1)}, s32[256]{0:T(256)}, u32[]{:S(2)}) copy-start(s32[256]{0:T(256)} %param.12) | copy-start | bytes 3076
  19.8 12.0 %copy-start.3 = (f32[256,6]{0,1:T(8,128)S(1)}, f32[256,6]{0,1:T(8,128)}, u32[]{:S(2)}) copy-start(f32[256,6]{0,1:T(8,128)} %param.10) | copy-start | bytes 18436
  82.3 32.6 %copy-start.5 = (s32[32]{0:T(128)S(1)}, s32[32]{0:T(128)}, u32[]{:S(2)}) copy-start(s32[32]{0:T(128)} %param.13) | copy-start | bytes 388
  91.5 25.1 %copy-start.2 = (f32[2,4096]{1,0:T(2,128)}, f32[2,4096]{1,0:T(2,128)S(1)}, u32[]{:S(2)}) copy-start(f32[2,4096]{1,0:T(2,128)S(1)} %mul.83) | copy-start | bytes 98308
Sparse Core Ops, SparseCore 0:
  10.3 64.5 all-gather.2
where the time goes:
time: 124 us; the launch traced here: 123 us
  local copies, waits for them, and re-layouts  42 us (34%)
  waiting for transfers between devices  30.3 us (24%)
  blocking collectives  22 us (18%)
  between operations  14.2 us (11%)
  matrix products  12.8 us (10%)
  other arithmetic  2.08 us (2%)
    all_gather x1, waiting for transfers between devices, on_device(): lax.all_gather(in_factor, 'expert', axis=0, tiled=True)  29.6 us
    all_gather x1, blocking collectives, on_device(): pieces = lax.all_gather(sketch, 'expert', axis=0, tiled=True)  22 us
    scatter x1, local copies, waits for them, and re-layouts, on_device(): hidden_buffer.at[slot_place].set(hidden.reshape(slot_count, feat_width))  12.4 us
    unnamed x17, local copies, waits for them, and re-layouts  10.2 us
    reshape x1, local copies, waits for them, and re-layouts, on_device(): hidden.reshape(slot_count, feat_width)  8.53 us
    dot_general x1, matrix products, on_device(): jnp.einsum('ecf,efk->eck', hidden_buffer, lax.all_gather(in_factor, 'expe...  7.43 us
    gather x2, local copies, waits for them, and re-layouts, on_device(): slot_proj = in_proj.reshape(experts_all * capacity, rank_width)[slot_place]  7.02 us
  transfers between devices with their start and end apart: 1, of which 1 were waited for; matrix products, arithmetic and copies ran while one was open for 30% of the time, Pallas kernels for 0%

commit v1 on v0

v1 whole, which is shorter than its diff:
```python
import functools

import jax
import jax.numpy as jnp
from jax import lax
from jax.experimental import pallas as pl
from jax.experimental.pallas import tpu as pltpu
from jax.sharding import PartitionSpec as P

EX_DEV = 2
PARTS = 3

sketch_scale = 0.125
score_scale = 1.0 / 512.0
epsilon = 1e-06

MESH = pl.DeviceIdType.MESH
HIGHEST = lax.Precision.HIGHEST
NT = (((1,), (1,)), ((), ()))


def kernel(
    n, hid_hbm, og_hbm, of_hbm, w_hbm, info_ref, qcol_ref,
    sketch_ref, scores_ref,
    wall, x_ref, og_ref, of_ref, ids_ref, gate_ref, acc_ref, gm_ref,
    part_out, part_in, gram_out, gram_in,
    send_sem, recv_sem, local_sem, s1_send, s1_recv, s2_send, s2_recv,
):
    g = lax.axis_index("groups")
    e = lax.axis_index("expert")
    zn = n // 4
    core = e % 2
    y = (e // 2) % 2
    z = e // 4
    tokens = gm_ref.shape[0]
    top = x_ref.shape[0] // tokens
    width = wall.shape[3]
    half = part_out.shape[0]

    own_loads = [
        pltpu.make_async_copy(
            w_hbm.at[:, p * width : (p + 1) * width], wall.at[e, p], local_sem.at[p]
        )
        for p in range(PARTS)
    ]
    og_load = pltpu.make_async_copy(og_hbm, og_ref, local_sem.at[3])
    of_load = pltpu.make_async_copy(of_hbm, of_ref, local_sem.at[4])
    x_load = pltpu.make_async_copy(hid_hbm, x_ref, local_sem.at[5])
    for load in own_loads + [og_load, of_load, x_load]:
        load.start()

    barrier = pltpu.get_barrier_semaphore()
    g_other = g + 1 - 2 * (g % 2)

    def greet(off, carry):
        pl.semaphore_signal(
            barrier, inc=1, device_id=(g, lax.rem(e + off, n)), device_id_type=MESH
        )
        return carry

    lax.fori_loop(1, n, greet, 0)
    pl.semaphore_signal(barrier, inc=1, device_id=(g_other, e), device_id_type=MESH)
    pl.semaphore_wait(barrier, n)

    mine = 2 * (g % 2)
    theirs = 2 - mine

    def shard(col, zz, cc):
        return (zz * 2 + col) * 2 + cc

    up = (g, shard(y, jnp.minimum(z + 1, zn - 1), core))
    down = (g, shard(y, jnp.maximum(z - 1, 0), core))
    across = (g, shard(1 - y, z, core))
    other_x = (g_other, e)
    sibling = (g, shard(y, z, 1 - core))
    targets = (up, down, across, other_x, sibling)
    UP, DOWN, ACROSS, OTHER_X, SIBLING = range(5)

    def copy(kind, s, p):
        return pltpu.make_async_remote_copy(
            src_ref=wall.at[s, p],
            dst_ref=wall.at[s, p],
            send_sem=send_sem.at[kind, s // 2, p],
            recv_sem=recv_sem.at[s, p],
            device_id=targets[kind],
            device_id_type=MESH,
        )

    def arrived(s, p):
        copy(SIBLING, s, p).wait_recv()

    for load in own_loads:
        load.wait()

    def own_sends(act):
        for p in (mine, 1):
            act(ACROSS, e, p)
            pl.when(z + 1 < zn)(lambda p=p: act(UP, e, p))
            pl.when(z >= 1)(lambda p=p: act(DOWN, e, p))
        for p in range(PARTS):
            act(SIBLING, e, p)

    def start(kind, s, p):
        copy(kind, s, p).start()

    def finish(kind, s, p):
        copy(kind, s, p).wait_send()

    own_sends(start)

    table = jnp.transpose(info_ref[...])
    lane = lax.broadcasted_iota(jnp.int32, (tokens, 128), 1)
    upper = lane >= 64
    upper_f = upper.astype(jnp.float32)
    for k in range(top):
        rows = pl.ds(k * tokens, tokens)
        ids_ref[rows, :] = jnp.broadcast_to(table[:, k : k + 1], (tokens, 128)) - upper_f
        gate_ref[rows, :] = jnp.broadcast_to(table[:, top + k : top + k + 1], (tokens, 128))
    example = jnp.broadcast_to(table[:, 2 * top : 2 * top + 1], (tokens, 128))
    acc_ref[...] = jnp.zeros_like(acc_ref)
    gram_out[...] = jnp.zeros_like(gram_out)
    og_load.wait()
    of_load.wait()
    factor = of_ref[...]
    proj = lax.dot_general(
        og_ref[...], jnp.concatenate([factor, factor], axis=0), NT,
        preferred_element_type=jnp.float32,
    )
    gm_ref[...] = jnp.where(example == upper_f, proj * sketch_scale, 0.0)
    x_load.wait()

    def from_z(r, act):
        for kind, zs, onward in ((UP, z - r, z + 1 < zn), (DOWN, z + r, z >= 1)):

            @pl.when((zs >= 0) & (zs < zn))
            def _(kind=kind, zs=zs, onward=onward):
                s = shard(y, zs, core)
                for p in (mine, 1):
                    if act is start:
                        arrived(s, p)
                    pl.when(onward)(lambda p=p: act(kind, s, p))
                    act(ACROSS, s, p)
                    if p is mine:
                        act(OTHER_X, s, p)
                    act(SIBLING, s, p)

    def from_y(r, act):
        def one(i, carry):
            zs = z + r * (2 * i - 1)

            @pl.when((zs >= 0) & (zs < zn) & ((r > 0) | (i == 0)))
            def _():
                s = shard(1 - y, zs, core)
                for p in (mine, 1):
                    if act is start:
                        arrived(s, p)
                    if p is mine:
                        act(OTHER_X, s, p)
                    act(SIBLING, s, p)

            return carry

        lax.fori_loop(0, 2, one, 0)

    def from_x(r, act):
        def one(i, carry):
            zs = z + r * (2 * (i // 2) - 1)
            col = i % 2

            @pl.when((zs >= 0) & (zs < zn) & ((r > 0) | ((i // 2 == 0) & (col != y))))
            def _():
                s = shard(col, zs, core)
                if act is start:
                    arrived(s, theirs)
                act(SIBLING, s, theirs)

            return carry

        lax.fori_loop(0, 4, one, 0)

    def compute(r):
        def one(i, carry):
            zs = z + r * (2 * (i // 2) - 1)
            col = i % 2

            @pl.when((zs >= 0) & (zs < zn) & ((r > 0) | (i // 2 == 0)))
            def _():
                place = zs * 2 + col
                for p in range(PARTS):
                    arrived(place * 2 + 1 - core, p)
                weights = jnp.concatenate(
                    [
                        jnp.concatenate([wall[2 * place + h, p] for p in range(PARTS)], axis=1)
                        for h in range(2)
                    ],
                    axis=0,
                )
                prod = lax.dot_general(
                    x_ref[...], weights, NT, preferred_element_type=jnp.float32
                )
                first = (4 * place).astype(jnp.float32)
                total = acc_ref[...]
                for k in range(top):
                    rows = slice(k * tokens, (k + 1) * tokens)
                    ids = ids_ref[rows, :]
                    chosen = jnp.where(
                        ids == first,
                        prod[rows, :128],
                        jnp.where(ids == first + 2.0, prod[rows, 128:], 0.0),
                    )
                    total = total + gate_ref[rows, :] * chosen
                acc_ref[...] = total

            return carry

        lax.fori_loop(0, 4, one, 0)

    def step(t, carry):
        pl.when(t + 1 < zn)(lambda: from_z(t + 1, start))
        pl.when(t < zn)(lambda: from_y(t, start))
        pl.when(t >= 1)(lambda: compute(t - 1))
        pl.when(t < zn)(lambda: from_x(t, start))
        return carry

    lax.fori_loop(0, zn + 1, step, 0)

    pre = lax.dot_general(
        jnp.transpose(acc_ref[...]), gm_ref[...], (((1,), (0,)), ((), ())),
        precision=HIGHEST, preferred_element_type=jnp.float32,
    )
    sk = pre[:64] + pre[64:]
    sketch_ref[...] = sk
    rows_each = part_out.shape[1]
    for d in range(n):
        part_out[d] = sk[d * rows_each : (d + 1) * rows_each]

    def exchange(src, dst, send, recv, off):
        to = lax.rem(e + off, n)
        return pltpu.make_async_remote_copy(
            src_ref=src.at[to], dst_ref=dst.at[e],
            send_sem=send.at[to], recv_sem=recv.at[e],
            device_id=(g, to), device_id_type=MESH,
        )

    def incoming(src, dst, send, recv, off):
        frm = lax.rem(e + off, n)
        return pltpu.make_async_remote_copy(
            src_ref=src.at[frm], dst_ref=dst.at[frm],
            send_sem=send.at[frm], recv_sem=recv.at[frm],
            device_id=(g, frm), device_id_type=MESH,
        )

    def every(act):
        def one(off, carry):
            act(off)
            return carry

        lax.fori_loop(1, n, one, 0)

    one_set = (part_out, part_in, s1_send, s1_recv)
    two_set = (gram_out, gram_in, s2_send, s2_recv)
    every(lambda off: exchange(*one_set, off).start())
    part_in[e] = part_out[e]
    every(lambda off: incoming(*one_set, off).wait_recv())

    slabs = [part_in[:, i, :] for i in range(rows_each)]
    zmat = jnp.concatenate(
        [
            jnp.concatenate([slab[:, :64] for slab in slabs], axis=1),
            jnp.concatenate([slab[:, 64:] for slab in slabs], axis=1),
        ],
        axis=0,
    )
    gram = lax.dot_general(
        zmat, zmat, NT, precision=HIGHEST, preferred_element_type=jnp.float32
    )
    pairs = 2 * half
    eye = lax.broadcasted_iota(jnp.int32, (pairs, pairs), 0) == lax.broadcasted_iota(
        jnp.int32, (pairs, pairs), 1
    )
    diag = jnp.sum(jnp.where(eye, gram, 0.0), axis=0, keepdims=True)
    gram_out[:, 0, :pairs] = gram[:half]
    gram_out[:, 1, :pairs] = gram[half:]
    gram_out[:, 2, :pairs] = jnp.broadcast_to(diag, (half, pairs))
    every(lambda off: exchange(*two_set, off).start())
    gram_in[e] = gram_out[e]
    every(lambda off: incoming(*two_set, off).wait_recv())
    total = jnp.sum(gram_in[...], axis=0)

    count = qcol_ref.shape[1]
    pick = (
        lax.broadcasted_iota(jnp.int32, (128, count), 0)
        == jnp.broadcast_to(qcol_ref[...], (128, count))
    ).astype(jnp.float32)
    raw = jnp.dot(total, pick, precision=HIGHEST, preferred_element_type=jnp.float32)
    size = sk.shape[0] * 64
    query_scale = lax.rsqrt(raw[2:3] * (1.0 / size) + epsilon)
    place = lax.broadcasted_iota(jnp.int32, (2, 128), 0) * n + e
    own = lax.broadcasted_iota(jnp.int32, (2, 128), 1) == place
    norm = jnp.sum(jnp.where(own, total[0:2], 0.0), axis=1, keepdims=True)
    row_scale = lax.rsqrt(norm * (1.0 / size) + epsilon)
    scores_ref[...] = raw[0:2] * row_scale * query_scale * score_scale

    own_sends(finish)

    def drain(r, carry):
        pl.when(r >= 1)(lambda: from_z(r, finish))
        from_y(r, finish)
        from_x(r, finish)
        return carry

    lax.fori_loop(0, zn, drain, 0)
    every(lambda off: exchange(*one_set, off).wait_send())
    every(lambda off: exchange(*two_set, off).wait_send())


def on_device(
    hidden, out_grad, gate_weights, expert_ids, example_ids, query_ids, in_factor, out_factor
):
    n = lax.axis_size("expert")
    tokens, top, feat = hidden.shape
    exp_local = in_factor.shape[0]
    rank = out_factor.shape[1]
    model = out_grad.shape[1]
    queries = query_ids.shape[0]
    hid = jnp.transpose(hidden, (1, 0, 2)).reshape(top * tokens, feat)
    w = jnp.transpose(in_factor, (0, 2, 1)).reshape(exp_local * rank, feat)
    factor = out_factor.T
    info = jnp.concatenate(
        [
            expert_ids.T.astype(jnp.float32),
            gate_weights.T,
            (example_ids % EX_DEV).astype(jnp.float32)[None, :],
            jnp.zeros((16 - 2 * top - 1, tokens), jnp.float32),
        ],
        axis=0,
    )
    qcol = ((query_ids % EX_DEV) * n + query_ids // EX_DEV)[None, :]
    any_spec = pl.BlockSpec(memory_space=pl.ANY)
    vmem = pl.BlockSpec(memory_space=pltpu.VMEM)
    rows_each = rank // n
    f32, bf16 = jnp.float32, jnp.bfloat16
    sketch, scores = pl.pallas_call(
        functools.partial(kernel, n),
        out_shape=(
            jax.ShapeDtypeStruct((rank, EX_DEV * rank), f32),
            jax.ShapeDtypeStruct((EX_DEV, queries), f32),
        ),
        in_specs=[any_spec] * 4 + [vmem] * 2,
        out_specs=(vmem, vmem),
        scratch_shapes=[
            pltpu.VMEM((n, PARTS, exp_local * rank, feat // PARTS), bf16),
            pltpu.VMEM((top * tokens, feat), bf16),
            pltpu.VMEM((tokens, model), bf16),
            pltpu.VMEM((rank, model), bf16),
            pltpu.VMEM((top * tokens, 128), f32),
            pltpu.VMEM((top * tokens, 128), f32),
            pltpu.VMEM((tokens, 128), f32),
            pltpu.VMEM((tokens, 128), f32),
            pltpu.VMEM((n, rows_each, 128), f32),
            pltpu.VMEM((n, rows_each, 128), f32),
            pltpu.VMEM((n, 8, 128), f32),
            pltpu.VMEM((n, 8, 128), f32),
            pltpu.SemaphoreType.DMA((5, n // 2, PARTS)),
            pltpu.SemaphoreType.DMA((n, PARTS)),
            pltpu.SemaphoreType.DMA((6,)),
            pltpu.SemaphoreType.DMA((n,)),
            pltpu.SemaphoreType.DMA((n,)),
            pltpu.SemaphoreType.DMA((n,)),
            pltpu.SemaphoreType.DMA((n,)),
        ],
        compiler_params=pltpu.CompilerParams(
            collective_id=0, has_side_effects=True, vmem_limit_bytes=52 * 1024 * 1024
        ),
    )(hid, out_grad, factor, w, info, qcol)
    sketch = jnp.transpose(sketch.reshape(rank, EX_DEV, rank), (1, 0, 2))
    return (sketch.reshape(EX_DEV, rank * rank), scores)


def solution(mesh):
    in_specs = (
        P(("groups", "expert"), None, None),
        P(("groups", "expert"), None),
        P(("groups", "expert"), None),
        P(("groups", "expert"), None),
        P(("groups", "expert")),
        P("groups"),
        P("expert", None, None),
        P(),
    )
    out_specs = (P(("groups", "expert"), None), P(("groups", "expert"), None))
    return jax.shard_map(
        on_device, mesh=mesh, in_specs=in_specs, out_specs=out_specs, check_vma=False
    )
```

time: 124 us -> 59.9 us (0.48)
  Pallas kernels: 0 us -> 52.6 us
  local copies, waits for them, and re-layouts: 42 us -> 3.53 us
  waiting for transfers between devices: 30.3 us -> 0 us
  blocking collectives: 22 us -> 0 us
  between operations: 14.2 us -> 0.66 us
  matrix products: 12.8 us -> 0 us
    pallas_call x0 -> x1, Pallas kernels: none -> 52.6 us  [on_device(): pl.pallas_call(functools.partial(kernel, n), out_shape=(jax.ShapeDtypeStr...]
    all_gather x1 -> x0, waiting for transfers between devices: 29.6 us -> none  [on_device(): lax.all_gather(in_factor, 'expert', axis=0, tiled=True)]
    all_gather x1 -> x0, blocking collectives: 22 us -> none  [on_device(): pieces = lax.all_gather(sketch, 'expert', axis=0, tiled=True)]
    dot_general x6 -> x0, matrix products: 12.8 us -> none  [the longest x1 7.43 us: on_device(): jnp.einsum('ecf,efk->eck', hidden_buffer, lax.all_gather(in_factor, 'expe...]
    scatter x1 -> x0, local copies, waits for them, and re-layouts: 12.4 us -> none  [on_device(): hidden_buffer.at[slot_place].set(hidden.reshape(slot_count, feat_width))]
    reshape x2, local copies, waits for them, and re-layouts: 9.85 us -> 0.8 us  [the longest x1 0.71 us: on_device(): return (sketch.reshape(EX_DEV, rank * rank), scores)]
    unnamed x17 -> x5, local copies, waits for them, and re-layouts: 10.2 us -> 2.64 us
    gather x2 -> x0, local copies, waits for them, and re-layouts: 7.02 us -> none  [on_device(): slot_proj = in_proj.reshape(experts_all * capacity, rank_width)[slot_place]]
  transfers between devices with their start and end apart: 1 -> 0, of which waited for: 1 -> 0; matrix products, arithmetic and copies ran while one was open for 30% -> 0% of each run, Pallas kernels for 0% -> 0%
where the time goes in v1:
time: 59.9 us; the launch traced here: 59.6 us
  Pallas kernels  52.6 us (88%)
  local copies, waits for them, and re-layouts  3.53 us (6%)
  other arithmetic  2.82 us (5%)
  between operations  0.66 us (1%)
    pallas_call x1, Pallas kernels, on_device(): pl.pallas_call(functools.partial(kernel, n), out_shape=(jax.ShapeDtypeStr...  52.6 us
    unnamed x5, local copies, waits for them, and re-layouts  2.64 us

profile of v1, /device:TPU:0, one launch (start us, length us, event | category | flops | bytes accessed | tf_op | source)
XLA Modules:
  0.0 59.6 jit_solution(15978104141120714031)
XLA Ops:
  0.6 0.7 %fusion.4.qcol_ref = s32[1,32]{1,0:T(1,128)S(1)} fusion(s32[32]{0:T(128)} %param.13), kind=kLoop, calls=%fused_computation.14 | loop fusion | flops 672 | bytes 256 | tf_op jit(solution)/shard_map/broadcast_in_dim | solution.py:338
  1.3 0.1 pad.3.clone
  1.4 0.7 %fusion = f32[256]{0:T(256)S(1)} fusion(s32[256]{0:T(256)} %param.12), kind=kLoop, calls=%fused_computation.10 | loop fusion | flops 3072 | bytes 2048 | tf_op jit(solution)/shard_map/convert_element_type | solution.py:333
  2.1 0.7 %convert_bitcast_fusion = f32[6,256]{1,0:T(8,128)S(1)} fusion(s32[256,6]{0,1:T(8,128)} %param.11), kind=kLoop, calls=%fused_computation.1 | loop fusion | flops 1536 | bytes 12288 | tf_op jit(solution)/shard_map/convert_element_type | solution.py:331
  2.8 0.8 %maximum_maximum_fusion.info_ref = f32[16,256]{1,0:T(8,128)S(1)} fusion(f32[1,256]{1,0:T(1,128)S(1)} %bitcast.19, f32[6,256]{1,0:T(8,128)} %bitcast.18, f32[6,256]{1,0:T(8,128)S(1)} %convert_bitcast_fusion, f32[16]{0:T(128)S(1)} %pad.3.clone), kind=kLoop, calls=%fused_computation | loop fusion | flops 12288 | bytes 29760 | tf_op jit(solution)/shard_map/concatenate | solution.py:329
  3.5 0.0 copy-start
  3.5 1.1 %copy-done = bf16[5120,64]{0,1:T(8,128)(2,1)S(1)} copy-done((bf16[5120,64]{0,1:T(8,128)(2,1)S(1)}, bf16[5120,64]{0,1:T(8,128)(2,1)}, u32[]{:S(2)}) %copy-start) | copy-done | bytes 655384
  4.6 0.0 copy-start.1
  4.6 1.0 %copy-done.1 = bf16[2,1536,64]{1,2,0:T(8,128)(2,1)S(1)} copy-done((bf16[2,1536,64]{1,2,0:T(8,128)(2,1)S(1)}, bf16[2,1536,64]{1,2,0:T(8,128)(2,1)}, u32[]{:S(2)}) %copy-start.1) | copy-done | bytes 393240
  5.6 52.6 %shard_map.95 = (f32[64,128]{1,0:T(8,128)S(1)}, f32[2,32]{1,0:T(2,128)S(1)}) custom-call(bf16[1536,1536]{1,0:T(8,128)(2,1)} %bitcast.16, bf16[256,5120]{1,0:T(8,128)(2,1)} %og_hbm.1, bf16[64,5120]{1,0:T(8,128)(2,1)S(1)} %bitcast.14, bf16[128,1536]{1,0:T(8,128)(2,1)S(1)} %bitcast.15, f32[16,256]{1,0:T(8,128)S(1)} %maximum_maximum_fusion.info_ref, ...), custom_call_target="tpu_custom_call" | custom-call | tf_op jit(solution)/shard_map/pallas_call | solution.py:343
  58.2 0.1 reshape.18
  58.3 0.7 %reshape.19 = f32[2,4096]{1,0:T(2,128)} reshape(f32[2,64,64]{2,1,0:T(8,128)S(1)} %copy.10) | data formatting | bytes 65536 | tf_op jit(solution)/shard_map/reshape | solution.py:377
  59.0 0.6 copy.12
  (2 shorter events, 0.0 us)
Async XLA Ops:
  3.5 1.1 %copy-start = (bf16[5120,64]{0,1:T(8,128)(2,1)S(1)}, bf16[5120,64]{0,1:T(8,128)(2,1)}, u32[]{:S(2)}) copy-start(bf16[5120,64]{0,1:T(8,128)(2,1)} %param.15) | copy-start | bytes 1966084
  4.6 1.0 %copy-start.1 = (bf16[2,1536,64]{1,2,0:T(8,128)(2,1)S(1)}, bf16[2,1536,64]{1,2,0:T(8,128)(2,1)}, u32[]{:S(2)}) copy-start(bf16[2,1536,64]{1,2,0:T(8,128)(2,1)} %param.14) | copy-start | bytes 1179652

commit v2 on v1

v2 whole, which is shorter than its diff:
```python
import functools

import jax
import jax.numpy as jnp
from jax import lax
from jax.experimental import pallas as pl
from jax.experimental.pallas import tpu as pltpu
from jax.sharding import PartitionSpec as P

EX_DEV = 2
PARTS = 3

sketch_scale = 0.125
score_scale = 1.0 / 512.0
epsilon = 1e-06

MESH = pl.DeviceIdType.MESH
HIGHEST = lax.Precision.HIGHEST
NT = (((1,), (1,)), ((), ()))


def kernel(
    n, hid_hbm, og_hbm, of_hbm, w_hbm, ids_hbm, gates_hbm, example_hbm, query_hbm,
    sketch_ref, scores_ref,
    ids_in, gates_in, example_in, query_in, info_ref, sk_ref,
    wall, x_ref, og_ref, of_ref, ids_ref, gate_ref, acc_ref, gm_ref,
    part_out, part_in, gram_out, gram_in,
    send_sem, recv_sem, local_sem, s1_send, s1_recv, s2_send, s2_recv,
):
    g = lax.axis_index("groups")
    e = lax.axis_index("expert")
    zn = n // 4
    core = e % 2
    y = (e // 2) % 2
    z = e // 4
    tokens = gm_ref.shape[0]
    top = x_ref.shape[0] // tokens
    width = wall.shape[3]
    half = part_out.shape[0]

    barrier = pltpu.get_barrier_semaphore()
    g_other = g + 1 - 2 * (g % 2)
    pl.semaphore_signal(barrier, inc=1, device_id=(g_other, e), device_id_type=MESH)

    def greet(off, carry):
        pl.semaphore_signal(
            barrier, inc=1, device_id=(g, lax.rem(e + off, n)), device_id_type=MESH
        )
        return carry

    lax.fori_loop(1, n, greet, 0)

    own_loads = [
        pltpu.make_async_copy(
            w_hbm.at[:, p * width : (p + 1) * width], wall.at[e, p], local_sem.at[p]
        )
        for p in range(PARTS)
    ]
    og_load = pltpu.make_async_copy(og_hbm, og_ref, local_sem.at[3])
    of_load = pltpu.make_async_copy(of_hbm, of_ref, local_sem.at[4])
    x_load = pltpu.make_async_copy(hid_hbm, x_ref, local_sem.at[5])
    small_loads = [
        pltpu.make_async_copy(src, dst, local_sem.at[6 + i])
        for i, (src, dst) in enumerate(
            (
                (ids_hbm, ids_in),
                (gates_hbm, gates_in),
                (example_hbm, example_in),
                (query_hbm, query_in),
            )
        )
    ]
    for load in own_loads + small_loads + [og_load, of_load, x_load]:
        load.start()
    info_ref[...] = jnp.zeros_like(info_ref)
    acc_ref[...] = jnp.zeros_like(acc_ref)
    gram_out[...] = jnp.zeros_like(gram_out)

    pl.semaphore_wait(barrier, n)

    mine = 2 * (g % 2)
    theirs = 2 - mine

    def shard(col, zz, cc):
        return (zz * 2 + col) * 2 + cc

    up = (g, shard(y, jnp.minimum(z + 1, zn - 1), core))
    down = (g, shard(y, jnp.maximum(z - 1, 0), core))
    across = (g, shard(1 - y, z, core))
    other_x = (g_other, e)
    sibling = (g, shard(y, z, 1 - core))
    targets = (up, down, across, other_x, sibling)
    UP, DOWN, ACROSS, OTHER_X, SIBLING = range(5)

    def copy(kind, s, p):
        return pltpu.make_async_remote_copy(
            src_ref=wall.at[s, p],
            dst_ref=wall.at[s, p],
            send_sem=send_sem.at[kind, s // 2, p],
            recv_sem=recv_sem.at[s, p],
            device_id=targets[kind],
            device_id_type=MESH,
        )

    def arrived(s, p):
        copy(SIBLING, s, p).wait_recv()

    for load in own_loads:
        load.wait()

    def own_sends(act):
        for p in (mine, 1):
            act(ACROSS, e, p)
            pl.when(z + 1 < zn)(lambda p=p: act(UP, e, p))
            pl.when(z >= 1)(lambda p=p: act(DOWN, e, p))
        for p in range(PARTS):
            act(SIBLING, e, p)

    def start(kind, s, p):
        copy(kind, s, p).start()

    def finish(kind, s, p):
        copy(kind, s, p).wait_send()

    own_sends(start)

    for load in small_loads:
        load.wait()
    info_ref[0:top, :] = ids_in[...].astype(jnp.float32)
    info_ref[top : 2 * top, :] = gates_in[...]
    info_ref[2 * top : 2 * top + 1, :] = lax.rem(example_in[...], EX_DEV).astype(jnp.float32)
    table = jnp.transpose(info_ref[...])
    lane = lax.broadcasted_iota(jnp.int32, (tokens, 128), 1)
    upper = lane >= 64
    upper_f = upper.astype(jnp.float32)
    for k in range(top):
        rows = pl.ds(k * tokens, tokens)
        ids_ref[rows, :] = jnp.broadcast_to(table[:, k : k + 1], (tokens, 128)) - upper_f
        gate_ref[rows, :] = jnp.broadcast_to(table[:, top + k : top + k + 1], (tokens, 128))
    example = jnp.broadcast_to(table[:, 2 * top : 2 * top + 1], (tokens, 128))
    og_load.wait()
    of_load.wait()
    factor = of_ref[...]
    proj = lax.dot_general(
        og_ref[...], jnp.concatenate([factor, factor], axis=0), NT,
        preferred_element_type=jnp.float32,
    )
    gm_ref[...] = jnp.where(example == upper_f, proj * sketch_scale, 0.0)
    x_load.wait()

    def from_z(r, p, act):
        for kind, zs, onward in ((UP, z - r, z + 1 < zn), (DOWN, z + r, z >= 1)):

            @pl.when((zs >= 0) & (zs < zn))
            def _(kind=kind, zs=zs, onward=onward):
                s = shard(y, zs, core)
                if act is start:
                    arrived(s, p)
                pl.when(onward)(lambda: act(kind, s, p))
                act(ACROSS, s, p)
                if p is mine:
                    act(OTHER_X, s, p)
                act(SIBLING, s, p)

    def at_distance(r, body):
        def one(i, carry):
            zs = z + r * (2 * i - 1)
            pl.when((zs >= 0) & (zs < zn) & ((r > 0) | (i == 0)))(lambda: body(zs))
            return carry

        lax.fori_loop(0, 2, one, 0)

    def from_y(r, p, act):
        def body(zs):
            s = shard(1 - y, zs, core)
            if act is start:
                arrived(s, p)
            if p is mine:
                act(OTHER_X, s, p)
            act(SIBLING, s, p)

        at_distance(r, body)

    def from_x(r, col, act):
        def body(zs):
            s = shard(col, zs, core)
            if act is start:
                arrived(s, theirs)
            act(SIBLING, s, theirs)

        at_distance(r, body)

    def compute(r, col):
        def body(zs):
            place = zs * 2 + col
            for p in range(PARTS):
                arrived(place * 2 + 1 - core, p)
            weights = jnp.concatenate(
                [
                    jnp.concatenate([wall[2 * place + h, p] for p in range(PARTS)], axis=1)
                    for h in range(2)
                ],
                axis=0,
            )
            prod = lax.dot_general(
                x_ref[...], weights, NT, preferred_element_type=jnp.float32
            )
            first = (4 * place).astype(jnp.float32)
            total = acc_ref[...]
            for k in range(top):
                rows = slice(k * tokens, (k + 1) * tokens)
                ids = ids_ref[rows, :]
                chosen = jnp.where(
                    ids == first,
                    prod[rows, :128],
                    jnp.where(ids == first + 2.0, prod[rows, 128:], 0.0),
                )
                total = total + gate_ref[rows, :] * chosen
            acc_ref[...] = total

        at_distance(r, body)

    def step(t, carry):
        further = t + 1 < zn
        inside = t < zn

        @pl.when(further)
        def _():
            from_z(t + 1, mine, start)

        @pl.when(inside)
        def _():
            from_y(t, mine, start)

        @pl.when(t >= 1)
        def _():
            from_x(t - 1, 1 - y, start)

        def product(half_step, carry):
            col = jnp.where(half_step == 0, y, 1 - y)
            r = t - half_step

            @pl.when((r >= 0) & (r < zn))
            def _():
                compute(r, col)

            @pl.when((half_step == 0) & further)
            def _():
                from_z(t + 1, 1, start)

            @pl.when((half_step == 0) & inside)
            def _():
                from_y(t, 1, start)

            @pl.when((half_step == 0) & further)
            def _():
                from_x(t + 1, y, start)

            return carry

        lax.fori_loop(0, 2, product, 0)
        return carry

    lax.fori_loop(0, zn + 1, step, 0)

    pre = lax.dot_general(
        jnp.transpose(acc_ref[...]), gm_ref[...], (((1,), (0,)), ((), ())),
        precision=HIGHEST, preferred_element_type=jnp.float32,
    )
    sk = pre[:64] + pre[64:]
    rows_each = part_out.shape[1]
    for d in range(n):
        part_out[d] = sk[d * rows_each : (d + 1) * rows_each]

    def exchange(src, dst, send, recv, off):
        to = lax.rem(e + off, n)
        return pltpu.make_async_remote_copy(
            src_ref=src.at[to], dst_ref=dst.at[e],
            send_sem=send.at[to], recv_sem=recv.at[e],
            device_id=(g, to), device_id_type=MESH,
        )

    def incoming(src, dst, send, recv, off):
        frm = lax.rem(e + off, n)
        return pltpu.make_async_remote_copy(
            src_ref=src.at[frm], dst_ref=dst.at[frm],
            send_sem=send.at[frm], recv_sem=recv.at[frm],
            device_id=(g, frm), device_id_type=MESH,
        )

    def every(act):
        def one(off, carry):
            act(off)
            return carry

        lax.fori_loop(1, n, one, 0)

    one_set = (part_out, part_in, s1_send, s1_recv)
    two_set = (gram_out, gram_in, s2_send, s2_recv)
    every(lambda off: exchange(*one_set, off).start())
    part_in[e] = part_out[e]

    sk_ref[...] = sk
    even = sk_ref[pl.ds(0, sk.shape[0] // 2, stride=2), :]
    odd = sk_ref[pl.ds(1, sk.shape[0] // 2, stride=2), :]
    low = lax.broadcasted_iota(jnp.int32, even.shape, 1) < 64
    sketch_ref[:, 0, :] = jnp.where(low, even, pltpu.roll(odd, 64, 1))
    sketch_ref[:, 1, :] = jnp.where(low, pltpu.roll(even, 64, 1), odd)
    own_sends(finish)

    def drain(r, carry):
        for p in (mine, 1):
            pl.when(r >= 1)(lambda p=p: from_z(r, p, finish))
            from_y(r, p, finish)
        from_x(r, 1 - y, finish)
        pl.when(r >= 1)(lambda: from_x(r, y, finish))
        return carry

    lax.fori_loop(0, zn, drain, 0)
    every(lambda off: incoming(*one_set, off).wait_recv())

    slabs = [part_in[:, i, :] for i in range(rows_each)]
    zmat = jnp.concatenate(
        [
            jnp.concatenate([slab[:, :64] for slab in slabs], axis=1),
            jnp.concatenate([slab[:, 64:] for slab in slabs], axis=1),
        ],
        axis=0,
    )
    gram = lax.dot_general(
        zmat, zmat, NT, precision=HIGHEST, preferred_element_type=jnp.float32
    )
    pairs = 2 * half
    eye = lax.broadcasted_iota(jnp.int32, (pairs, pairs), 0) == lax.broadcasted_iota(
        jnp.int32, (pairs, pairs), 1
    )
    diag = jnp.sum(jnp.where(eye, gram, 0.0), axis=0, keepdims=True)
    gram_out[:, 0, :pairs] = gram[:half]
    gram_out[:, 1, :pairs] = gram[half:]
    gram_out[:, 2, :pairs] = jnp.broadcast_to(diag, (half, pairs))
    every(lambda off: exchange(*two_set, off).start())
    gram_in[e] = gram_out[e]
    every(lambda off: exchange(*one_set, off).wait_send())
    every(lambda off: incoming(*two_set, off).wait_recv())
    total = jnp.sum(gram_in[...], axis=0)

    query = query_in[...]
    column = lax.rem(query, EX_DEV) * n + lax.div(query, EX_DEV)
    count = query.shape[1]
    pick = (
        lax.broadcasted_iota(jnp.int32, (128, count), 0)
        == jnp.broadcast_to(column, (128, count))
    ).astype(jnp.float32)
    raw = jnp.dot(total, pick, precision=HIGHEST, preferred_element_type=jnp.float32)
    size = sk.shape[0] * 64
    query_scale = lax.rsqrt(raw[2:3] * (1.0 / size) + epsilon)
    place = lax.broadcasted_iota(jnp.int32, (2, 128), 0) * n + e
    own = lax.broadcasted_iota(jnp.int32, (2, 128), 1) == place
    norm = jnp.sum(jnp.where(own, total[0:2], 0.0), axis=1, keepdims=True)
    row_scale = lax.rsqrt(norm * (1.0 / size) + epsilon)
    scores_ref[...] = raw[0:2] * row_scale * query_scale * score_scale

    every(lambda off: exchange(*two_set, off).wait_send())


def on_device(
    hidden, out_grad, gate_weights, expert_ids, example_ids, query_ids, in_factor, out_factor
):
    n = lax.axis_size("expert")
    tokens, top, feat = hidden.shape
    exp_local = in_factor.shape[0]
    rank = out_factor.shape[1]
    model = out_grad.shape[1]
    queries = query_ids.shape[0]
    hid = jnp.transpose(hidden, (1, 0, 2)).reshape(top * tokens, feat)
    w = jnp.transpose(in_factor, (0, 2, 1)).reshape(exp_local * rank, feat)
    factor = out_factor.T
    any_spec = pl.BlockSpec(memory_space=pl.ANY)
    vmem = pl.BlockSpec(memory_space=pltpu.VMEM)
    rows_each = rank // n
    f32, bf16 = jnp.float32, jnp.bfloat16
    sketch, scores = pl.pallas_call(
        functools.partial(kernel, n),
        out_shape=(
            jax.ShapeDtypeStruct((rank // 2, EX_DEV, 2 * rank), f32),
            jax.ShapeDtypeStruct((EX_DEV, queries), f32),
        ),
        in_specs=[any_spec] * 8,
        out_specs=(vmem, vmem),
        scratch_shapes=[
            pltpu.VMEM((top, tokens), jnp.int32),
            pltpu.VMEM((top, tokens), f32),
            pltpu.VMEM((1, tokens), jnp.int32),
            pltpu.VMEM((1, queries), jnp.int32),
            pltpu.VMEM((16, tokens), f32),
            pltpu.VMEM((rank, EX_DEV * rank), f32),
            pltpu.VMEM((n, PARTS, exp_local * rank, feat // PARTS), bf16),
            pltpu.VMEM((top * tokens, feat), bf16),
            pltpu.VMEM((tokens, model), bf16),
            pltpu.VMEM((rank, model), bf16),
            pltpu.VMEM((top * tokens, 128), f32),
            pltpu.VMEM((top * tokens, 128), f32),
            pltpu.VMEM((tokens, 128), f32),
            pltpu.VMEM((tokens, 128), f32),
            pltpu.VMEM((n, rows_each, 128), f32),
            pltpu.VMEM((n, rows_each, 128), f32),
            pltpu.VMEM((n, 8, 128), f32),
            pltpu.VMEM((n, 8, 128), f32),
            pltpu.SemaphoreType.DMA((5, n // 2, PARTS)),
            pltpu.SemaphoreType.DMA((n, PARTS)),
            pltpu.SemaphoreType.DMA((10,)),
            pltpu.SemaphoreType.DMA((n,)),
            pltpu.SemaphoreType.DMA((n,)),
            pltpu.SemaphoreType.DMA((n,)),
            pltpu.SemaphoreType.DMA((n,)),
        ],
        compiler_params=pltpu.CompilerParams(
            collective_id=0, has_side_effects=True, vmem_limit_bytes=60 * 1024 * 1024
        ),
    )(
        hid, out_grad, factor, w, expert_ids.T, gate_weights.T,
        example_ids[None, :], query_ids[None, :],
    )
    sketch = jnp.transpose(sketch, (1, 0, 2))
    return (sketch.reshape(EX_DEV, rank * rank), scores)


def solution(mesh):
    in_specs = (
        P(("groups", "expert"), None, None),
        P(("groups", "expert"), None),
        P(("groups", "expert"), None),
        P(("groups", "expert"), None),
        P(("groups", "expert")),
        P("groups"),
        P("expert", None, None),
        P(),
    )
    out_specs = (P(("groups", "expert"), None), P(("groups", "expert"), None))
    return jax.shard_map(
        on_device, mesh=mesh, in_specs=in_specs, out_specs=out_specs, check_vma=False
    )
```

time: 59.9 us -> 52.6 us (0.88)
  Pallas kernels: 52.6 us -> 49.2 us
  other arithmetic: 2.82 us -> 0 us
  local copies, waits for them, and re-layouts: 3.53 us -> 2.6 us
    pallas_call x1, Pallas kernels: 52.6 us -> 49.2 us  [on_device(): pl.pallas_call(functools.partial(kernel, n), out_shape=(jax.ShapeDtypeStr...]
    convert_element_type x2 -> x0, other arithmetic: 1.39 us -> none  [the longest x1 0.7 us: on_device(): expert_ids.T.astype(jnp.float32)]
    reshape x2 -> x0, local copies, waits for them, and re-layouts: 0.8 us -> none  [the longest x1 0.71 us: on_device(): return (sketch.reshape(EX_DEV, rank * rank), scores)]
    concatenate x1 -> x0, other arithmetic: 0.77 us -> none  [on_device(): jnp.concatenate([expert_ids.T.astype(jnp.float32), gate_weights.T, (examp...]
    broadcast_in_dim x1 -> x0, other arithmetic: 0.67 us -> none  [on_device(): qcol = (query_ids % EX_DEV * n + query_ids // EX_DEV)[None, :]]
    unnamed x5 -> x2, local copies, waits for them, and re-layouts: 2.64 us -> 2.6 us
where the time goes in v2:
time: 52.6 us; the launch traced here: 52.4 us
  Pallas kernels  49.2 us (94%)
  local copies, waits for them, and re-layouts  2.6 us (5%)
  between operations  0.64 us (1%)
    pallas_call x1, Pallas kernels, on_device(): pl.pallas_call(functools.partial(kernel, n), out_shape=(jax.ShapeDtypeStr...  49.2 us
    unnamed x2, local copies, waits for them, and re-layouts  2.6 us

profile of v2, /device:TPU:0, one launch (start us, length us, event | category | flops | bytes accessed | tf_op | source)
XLA Modules:
  0.0 52.4 jit_solution(9781491865061899257)
XLA Ops:
  0.6 49.2 %shard_map.95 = (f32[32,2,128]{2,1,0:T(2,128)}, f32[2,32]{1,0:T(2,128)}) custom-call(bf16[1536,1536]{1,0:T(8,128)(2,1)} %bitcast.14, bf16[256,5120]{1,0:T(8,128)(2,1)} %og_hbm.1, bf16[64,5120]{1,0:T(8,128)(2,1)} %bitcast.15, bf16[128,1536]{1,0:T(8,128)(2,1)} %bitcast.16, s32[6,256]{1,0:T(8,128)} %bitcast.18, f32[6,256]{1,0:T(8,128)} %bitcast.19, ...), custom_call_target="tpu_custom_call" | custom-call | tf_op jit(solution)/shard_map/pallas_call | solution.py:382
  49.8 1.4 %copy.12 = f32[2,4096]{1,0:T(2,128)} copy(f32[2,4096]{1,0:T(2,128)} %bitcast.17) | data formatting | bytes 65536
  51.2 1.2 %copy.13 = f32[2,32]{1,0:T(2,128)} copy(f32[2,32]{1,0:T(2,128)} %get-tuple-element.9) | data formatting | bytes 512

commit v3 on v2

--- a/solution.py
+++ b/solution.py
@@ -38,17 +38,24 @@
     width = wall.shape[3]
     half = part_out.shape[0]
 
+    def shard(col, zz, cc):
+        return (zz * 2 + col) * 2 + cc
+
     barrier = pltpu.get_barrier_semaphore()
     g_other = g + 1 - 2 * (g % 2)
     pl.semaphore_signal(barrier, inc=1, device_id=(g_other, e), device_id_type=MESH)
 
-    def greet(off, carry):
-        pl.semaphore_signal(
-            barrier, inc=1, device_id=(g, lax.rem(e + off, n)), device_id_type=MESH
-        )
-        return carry
-
-    lax.fori_loop(1, n, greet, 0)
+    for there, device in (
+        (z + 1 < zn, shard(y, jnp.minimum(z + 1, zn - 1), core)),
+        (z >= 1, shard(y, jnp.maximum(z - 1, 0), core)),
+    ):
+
+        @pl.when(there)
+        def _(device=device):
+            pl.semaphore_signal(barrier, inc=1, device_id=(g, device), device_id_type=MESH)
+
+    for device in (shard(1 - y, z, core), shard(y, z, 1 - core)):
+        pl.semaphore_signal(barrier, inc=1, device_id=(g, device), device_id_type=MESH)
 
     own_loads = [
         pltpu.make_async_copy(
@@ -76,13 +83,10 @@
     acc_ref[...] = jnp.zeros_like(acc_ref)
     gram_out[...] = jnp.zeros_like(gram_out)
 
-    pl.semaphore_wait(barrier, n)
+    pl.semaphore_wait(barrier, 3 + jnp.where(z + 1 < zn, 1, 0) + jnp.where(z >= 1, 1, 0))
 
     mine = 2 * (g % 2)
     theirs = 2 - mine
-
-    def shard(col, zz, cc):
-        return (zz * 2 + col) * 2 + cc
 
     up = (g, shard(y, jnp.minimum(z + 1, zn - 1), core))
     down = (g, shard(y, jnp.maximum(z - 1, 0), core))
@@ -244,11 +248,13 @@
             def _():
                 compute(r, col)
 
+            late = (t == zn - 1).astype(jnp.int32)
+
             @pl.when((half_step == 0) & further)
             def _():
                 from_z(t + 1, 1, start)
 
-            @pl.when((half_step == 0) & inside)
+            @pl.when((half_step == late) & inside)
             def _():
                 from_y(t, 1, start)
 

time: 52.6 us -> 49.1 us (0.933)
  Pallas kernels: 49.2 us -> 45.6 us
    pallas_call x1, Pallas kernels: 49.2 us -> 45.6 us  [on_device(): pl.pallas_call(functools.partial(kernel, n), out_shape=(jax.ShapeDtypeStr...]
where the time goes in v3:
time: 49.1 us; the launch traced here: 48.9 us
  Pallas kernels  45.6 us (93%)
  local copies, waits for them, and re-layouts  2.6 us (5%)
  between operations  0.64 us (1%)
    pallas_call x1, Pallas kernels, on_device(): pl.pallas_call(functools.partial(kernel, n), out_shape=(jax.ShapeDtypeStr...  45.6 us
    unnamed x2, local copies, waits for them, and re-layouts  2.6 us

profile of v3, /device:TPU:0, one launch (start us, length us, event | category | flops | bytes accessed | tf_op | source)
XLA Modules:
  0.0 48.9 jit_solution(14534019373592860572)
XLA Ops:
  0.6 45.6 %shard_map.95 = (f32[32,2,128]{2,1,0:T(2,128)}, f32[2,32]{1,0:T(2,128)}) custom-call(bf16[1536,1536]{1,0:T(8,128)(2,1)} %bitcast.14, bf16[256,5120]{1,0:T(8,128)(2,1)} %og_hbm.1, bf16[64,5120]{1,0:T(8,128)(2,1)} %bitcast.15, bf16[128,1536]{1,0:T(8,128)(2,1)} %bitcast.16, s32[6,256]{1,0:T(8,128)} %bitcast.18, f32[6,256]{1,0:T(8,128)} %bitcast.19, ...), custom_call_target="tpu_custom_call" | custom-call | tf_op jit(solution)/shard_map/pallas_call | solution.py:388
  46.3 1.4 %copy.12 = f32[2,4096]{1,0:T(2,128)} copy(f32[2,4096]{1,0:T(2,128)} %bitcast.17) | data formatting | bytes 65536
  47.7 1.2 %copy.13 = f32[2,32]{1,0:T(2,128)} copy(f32[2,32]{1,0:T(2,128)} %get-tuple-element.9) | data formatting | bytes 512
